TPU v7x, 256 devices: a whole 4x4x8 slice. The times are simulated.
256 devices in a mesh: row: 16 (over z_lo, y, core), col: 16 (over z_hi, x).
Axes of the slice: x: 4, y: 4, z: 8 (z_hi: 4, z_lo: 2; z = z_hi * 2 + z_lo), core: 2. Of those that a mesh axis runs over, the one named last changes fastest.
Arguments:
- source_desc: bfloat16 [32768, 64], P('row', 'col'), may hold values from -9 to 9
- target_desc: bfloat16 [32768, 64], P('col'), may hold values from -9 to 9
- source_mass: bfloat16 [32768], P('row'), may hold values from 0.099609375 to 10
- target_mass: bfloat16 [32768], P('col'), may hold values from 0.099609375 to 10
Outputs:
- cross_source: float32 [32768], P('row')
- cross_target: float32 [32768], P('col')
- self_source: float32 [32768], P('row')
- self_target: float32 [32768], P('col')
All inputs are finite; a program needn't handle non-finite values.
Results may differ from a plain program's by a relative error of at most 0.0003.
Values may be sent and summed in bfloat16 or wider, within the bound.
A program may use at most 64 MiB of HBM per device.

v0:
```python
import math
import jax
import jax.numpy as jnp
from jax import lax
from jax.sharding import PartitionSpec as P

ITERS = 2
EPSILON = 0.25
REACH = 1.0
DAMPING = 1.0 / (1.0 + EPSILON / REACH)


def half_norms(points):
    wide = points.astype(jnp.float32)
    return 0.5 * jnp.sum(wide * wide, axis=1)


def tile_stats(
    left_desc, right_desc, left_norm, right_norm, left_weight, right_weight, want_rows, want_cols
):
    count = left_desc.shape[0]
    block = math.gcd(512, count)
    blocks = count // block
    width = left_desc.shape[1]
    right_count = right_desc.shape[0]
    inputs = (
        left_desc.reshape(blocks, block, width),
        left_norm.reshape(blocks, block),
        left_weight.reshape(blocks, block),
    )

    def advance(carry, pieces):
        piece_desc, piece_norm, piece_weight = pieces
        product = lax.dot_general(
            piece_desc, right_desc, (((1,), (1,)), ((), ())), preferred_element_type=jnp.float32
        )
        scaled = (piece_norm[:, None] + right_norm[None, :] - product) / EPSILON
        emitted = ()
        if want_rows:
            row_score = right_weight[None, :] - scaled
            row_top = jnp.max(row_score, axis=1)
            row_total = jnp.sum(jnp.exp(row_score - row_top[:, None]), axis=1)
            emitted = (row_top, row_total)
        if want_cols:
            col_top, col_total = carry
            col_score = piece_weight[:, None] - scaled
            fresh_top = jnp.maximum(col_top, jnp.max(col_score, axis=0))
            col_total = col_total * jnp.exp(col_top - fresh_top) + jnp.sum(
                jnp.exp(col_score - fresh_top[None, :]), axis=0
            )
            carry = (fresh_top, col_total)
        return (carry, emitted)

    if want_cols:
        start = (
            jnp.full((right_count,), -jnp.inf, jnp.float32),
            jnp.zeros((right_count,), jnp.float32),
        )
    else:
        start = ()
    carry, emitted = lax.scan(advance, start, inputs)
    rows_out = (emitted[0].reshape(count), emitted[1].reshape(count)) if want_rows else None
    cols_out = carry if want_cols else None
    return (rows_out, cols_out)


def reduce_col(maxima, totals):
    merged_top = lax.pmax(maxima, "col")
    merged_total = lax.psum(totals * jnp.exp(maxima - merged_top), "col")
    return merged_top + jnp.log(merged_total)


def reduce_row(maxima, totals):
    merged_top = lax.pmax(maxima, "row")
    merged_total = lax.psum(totals * jnp.exp(maxima - merged_top), "row")
    return merged_top + jnp.log(merged_total)


def body(source_desc, target_desc, source_mass, target_mass):
    row_devices = lax.axis_size("row")
    col_devices = lax.axis_size("col")
    row_index = lax.axis_index("row")
    col_index = lax.axis_index("col")
    tile_count = source_mass.shape[0]
    source_part = tile_count // col_devices
    target_part = target_desc.shape[0] // row_devices
    mass_piece = lax.dynamic_slice_in_dim(source_mass, col_index * source_part, source_part, 0)
    source_rows = lax.all_gather(source_desc, "col", axis=1, tiled=True)
    desc_piece = lax.dynamic_slice_in_dim(source_rows, col_index * source_part, source_part, 0)
    source_cols, source_col_mass = (
        lax.all_gather(desc_piece, "row", axis=0, tiled=True),
        lax.all_gather(mass_piece, "row", axis=0, tiled=True),
    )
    target_piece = lax.dynamic_slice_in_dim(target_desc, row_index * target_part, target_part, 0)
    target_mass_piece = lax.dynamic_slice_in_dim(
        target_mass, row_index * target_part, target_part, 0
    )
    target_rows, target_row_mass = (
        lax.all_gather(target_piece, "col", axis=0, tiled=True),
        lax.all_gather(target_mass_piece, "col", axis=0, tiled=True),
    )
    source_log = jnp.log(source_mass.astype(jnp.float32))
    source_col_log = jnp.log(source_col_mass.astype(jnp.float32))
    target_log = jnp.log(target_mass.astype(jnp.float32))
    target_row_log = jnp.log(target_row_mass.astype(jnp.float32))
    source_row_norm = half_norms(source_rows)
    source_col_norm = half_norms(source_cols)
    target_col_norm = half_norms(target_desc)
    target_row_norm = half_norms(target_rows)
    cross_source = jnp.zeros((tile_count,), jnp.float32)
    cross_target = jnp.zeros((target_desc.shape[0],), jnp.float32)
    self_source = jnp.zeros((tile_count,), jnp.float32)
    self_target = jnp.zeros((target_desc.shape[0],), jnp.float32)
    source_view = jnp.zeros((source_cols.shape[0],), jnp.float32)
    target_view = jnp.zeros((target_rows.shape[0],), jnp.float32)
    for iteration in range(ITERS):
        mirror_work = iteration + 1 < ITERS
        cross_rows, cross_cols = tile_stats(
            source_rows,
            target_desc,
            source_row_norm,
            target_col_norm,
            source_log + cross_source / EPSILON,
            target_log + cross_target / EPSILON,
            True,
            True,
        )
        source_self_rows, source_self_cols = tile_stats(
            source_rows,
            source_cols,
            source_row_norm,
            source_col_norm,
            source_log + self_source / EPSILON,
            source_col_log + source_view / EPSILON,
            True,
            mirror_work,
        )
        target_self_rows, target_self_cols = tile_stats(
            target_rows,
            target_desc,
            target_row_norm,
            target_col_norm,
            target_row_log + target_view / EPSILON,
            target_log + self_target / EPSILON,
            mirror_work,
            True,
        )
        col_maxima = [cross_rows[0], source_self_rows[0]]
        col_totals = [cross_rows[1], source_self_rows[1]]
        row_maxima = [cross_cols[0], target_self_cols[0]]
        row_totals = [cross_cols[1], target_self_cols[1]]
        if mirror_work:
            col_maxima.append(target_self_rows[0])
            col_totals.append(target_self_rows[1])
            row_maxima.append(source_self_cols[0])
            row_totals.append(source_self_cols[1])
        col_logs = reduce_col(jnp.concatenate(col_maxima), jnp.concatenate(col_totals))
        row_logs = reduce_row(jnp.concatenate(row_maxima), jnp.concatenate(row_totals))
        target_count = target_desc.shape[0]
        cross_source = 0.5 * cross_source + 0.5 * DAMPING * (-EPSILON * col_logs[:tile_count])
        self_source = 0.5 * self_source + 0.5 * DAMPING * (
            -EPSILON * col_logs[tile_count : 2 * tile_count]
        )
        cross_target = 0.5 * cross_target + 0.5 * DAMPING * (-EPSILON * row_logs[:target_count])
        self_target = 0.5 * self_target + 0.5 * DAMPING * (
            -EPSILON * row_logs[target_count : 2 * target_count]
        )
        if mirror_work:
            target_view = 0.5 * target_view + 0.5 * DAMPING * (
                -EPSILON * col_logs[2 * tile_count :]
            )
            source_view = 0.5 * source_view + 0.5 * DAMPING * (
                -EPSILON * row_logs[2 * target_count :]
            )
    return (cross_source, cross_target, self_source, self_target)


def solution(mesh):
    return jax.shard_map(
        body,
        mesh=mesh,
        in_specs=(P("row", "col"), P("col", None), P("row"), P("col")),
        out_specs=(P("row"), P("col"), P("row"), P("col")),
        check_vma=False,
    )
```

profile of v0, /device:TPU:32, one launch (start us, length us, event | category | flops | bytes accessed | tf_op | source)
XLA Modules:
  0.0 824.4 jit_solution(18188859646712844108)
XLA Ops:
  0.6 47.2 %all-gather = bf16[16,4,2048]{2,1,0:T(4,128)(2,1)S(1)} all-gather(bf16[1,4,2048]{2,1,0:T(4,128)(2,1)} %bitcast.208), channel_id=1, replica_groups=mesh['row'=16,'col'=16] {'col'}, dimensions={0}, use_global_device_ids=true | all-gather | bytes 278528 | tf_op jit(solution)/shard_map/all_gather | solution.py:88
  47.9 20.2 %all_gather.16 = bf16[2048,64]{0,1:T(8,128)(2,1)S(1)} all-gather(bf16[128,64]{0,1:T(8,128)(2,1)S(1)} %dynamic-slice_bitcast_fusion), channel_id=1, replica_groups=mesh['row'=16,'col'=16] {'row'}, dimensions={0}, use_global_device_ids=true | all-gather | bytes 278528 | tf_op jit(solution)/shard_map/all_gather | solution.py:91
  69.3 16.1 %all-gather.1 = bf16[16,1,128]{2,1,0:T(2,128)(2,1)S(1)} all-gather(bf16[1,1,128]{2,1,0:T(2,128)(2,1)S(1)} %dynamic-slice_bitcast_fusion.2), channel_id=1, replica_groups=mesh['row'=16,'col'=16] {'row'}, dimensions={0}, use_global_device_ids=true | all-gather | bytes 4352 | tf_op jit(solution)/shard_map/all_gather | solution.py:92
  86.6 26.9 %while.95 = (s32[]{:T(128)}, f32[2048]{0:T(1024)S(1)}, f32[2048]{0:T(1024)S(1)}, f32[4,512]{1,0:T(4,128)S(1)}, f32[4,512]{1,0:T(4,128)S(1)}, /*index=5*/f32[4,51...) while((s32[]{:T(128)}, f32[2048]{0:T(1024)S(1)}, ...), condition=%wide.region_14.15_spmd.clone, body=%wide.region_9.14_spmd.clone.sunk | while | flops 147858432 | bytes 9203864 | solution.py:61
  89.8 3.4 exponential_reduce_fusion.18
  96.5 3.4 exponential_reduce_fusion.18
  103.3 3.4 exponential_reduce_fusion.18
  110.0 3.4 exponential_reduce_fusion.18
  113.7 26.7 %while.94 = (s32[]{:T(128)}, f32[2048]{0:T(1024)S(1)}, f32[2048]{0:T(1024)S(1)}, f32[4,512]{1,0:T(4,128)S(1)}, f32[4,512]{1,0:T(4,128)S(1)}, /*index=5*/f32[4,51...) while((s32[]{:T(128)}, f32[2048]{0:T(1024)S(1)}, ...), condition=%wide.region_7.8_spmd.clone, body=%wide.region_2.7_spmd.clone.sunk | while | flops 147858432 | bytes 8941720 | solution.py:61
  136.9 3.4 exponential_reduce_fusion.17
  140.5 39.3 %all_gather.19 = bf16[2048,64]{0,1:T(8,128)(2,1)S(1)} all-gather(bf16[128,64]{0,1:T(8,128)(2,1)S(1)} %constant_dynamic-slice_fusion.11), channel_id=1, replica_groups=mesh['row'=16,'col'=16] {'col'}, dimensions={0}, use_global_device_ids=true | all-gather | bytes 278528 | tf_op jit(solution)/shard_map/all_gather | solution.py:99
  180.3 39.8 %all-gather.2 = bf16[16,1,128]{2,1,0:T(2,128)(2,1)S(1)} all-gather(bf16[1,1,128]{2,1,0:T(2,128)(2,1)S(1)} %dynamic-slice_bitcast_fusion.1), channel_id=1, replica_groups=mesh['row'=16,'col'=16] {'col'}, dimensions={0}, use_global_device_ids=true | all-gather | bytes 4352 | tf_op jit(solution)/shard_map/all_gather | solution.py:100
  220.2 26.7 %while.96 = (s32[]{:T(128)}, f32[2048]{0:T(1024)S(1)}, f32[2048]{0:T(1024)S(1)}, f32[4,512]{1,0:T(4,128)S(1)}, f32[4,512]{1,0:T(4,128)S(1)}, /*index=5*/f32[4,51...) while((s32[]{:T(128)}, f32[2048]{0:T(1024)S(1)}, ...), condition=%wide.region_21.22_spmd.clone, body=%wide.region_16.21_spmd.clone.sunk | while | flops 147858432 | bytes 8941720 | solution.py:61
  246.9 76.7 %pmax.28 = f32[6144]{0:T(1024)S(1)} all-reduce(f32[6144]{0:T(1024)S(1)} %constant_dynamic-update-slice_fusion.8), channel_id=1, replica_groups=mesh['row'=16,'col'=16] {'col'}, use_global_device_ids=true, to_apply=%region_22.23 | all-reduce | flops 6144 | bytes 49152 | tf_op jit(solution)/shard_map/pmax | solution.py:68
  323.7 76.7 %psum.28 = f32[6144]{0:T(1024)S(1)} all-reduce(f32[6144]{0:T(1024)S(1)} %maximum_multiply_fusion), channel_id=1, replica_groups=mesh['row'=16,'col'=16] {'col'}, use_global_device_ids=true, to_apply=%region_23.24 | all-reduce | flops 6144 | bytes 49152 | tf_op jit(solution)/shard_map/psum | solution.py:69
  400.5 22.8 %while.98 = (s32[]{:T(128)}, f32[2048]{0:T(1024)S(1)}, f32[2048]{0:T(1024)S(1)}, f32[4,512]{1,0:T(4,128)S(1)}, f32[4,512]{1,0:T(4,128)S(1)}, /*index=5*/f32[2048...) while((s32[]{:T(128)}, f32[2048]{0:T(1024)S(1)}, ...), condition=%wide.region_41.42_spmd.clone, body=%wide.region_38.0_spmd.clone.sunk | while | flops 141568000 | bytes 8908920 | solution.py:61
  423.3 53.0 %pmax.29 = f32[6144]{0:T(1024)S(1)} all-reduce(f32[6144]{0:T(1024)S(1)} %constant_dynamic-update-slice_fusion.9), channel_id=1, replica_groups=mesh['row'=16,'col'=16] {'row'}, use_global_device_ids=true, to_apply=%region_24.25 | all-reduce | flops 6144 | bytes 49152 | tf_op jit(solution)/shard_map/pmax | solution.py:74
  476.3 53.1 %psum.29 = f32[6144]{0:T(1024)S(1)} all-reduce(f32[6144]{0:T(1024)S(1)} %maximum_multiply_fusion.1), channel_id=1, replica_groups=mesh['row'=16,'col'=16] {'row'}, use_global_device_ids=true, to_apply=%region_25.26 | all-reduce | flops 6144 | bytes 49152 | tf_op jit(solution)/shard_map/psum | solution.py:75
  529.5 26.7 %while.97 = (s32[]{:T(128)}, f32[2048]{0:T(1024)S(1)}, f32[2048]{0:T(1024)S(1)}, f32[4,512]{1,0:T(4,128)S(1)}, f32[4,512]{1,0:T(4,128)S(1)}, /*index=5*/f32[4,51...) while((s32[]{:T(128)}, f32[2048]{0:T(1024)S(1)}, ...), condition=%wide.region_31.32_spmd.clone, body=%wide.region_26.31_spmd.clone.sunk | while | flops 147858432 | bytes 8941720 | solution.py:61
  556.3 52.9 %pmax.31 = f32[4096]{0:T(1024)S(1)} all-reduce(f32[4096]{0:T(1024)S(1)} %constant_dynamic-update-slice_fusion.3), channel_id=1, replica_groups=mesh['row'=16,'col'=16] {'row'}, use_global_device_ids=true, to_apply=%region_42.43 | all-reduce | flops 4096 | bytes 32768 | tf_op jit(solution)/shard_map/pmax | solution.py:74
  609.2 52.9 %psum.31 = f32[4096]{0:T(1024)S(1)} all-reduce(f32[4096]{0:T(1024)S(1)} %maximum_multiply_fusion.3), channel_id=1, replica_groups=mesh['row'=16,'col'=16] {'row'}, use_global_device_ids=true, to_apply=%region_43.44 | all-reduce | flops 4096 | bytes 32768 | tf_op jit(solution)/shard_map/psum | solution.py:75
  662.8 7.4 while.93
  670.3 76.7 %pmax.30 = f32[4096]{0:T(1024)S(1)} all-reduce(f32[4096]{0:T(1024)S(1)} %constant_dynamic-update-slice_fusion.2), channel_id=1, replica_groups=mesh['row'=16,'col'=16] {'col'}, use_global_device_ids=true, to_apply=%region_36.37 | all-reduce | flops 4096 | bytes 32768 | tf_op jit(solution)/shard_map/pmax | solution.py:68
  747.0 76.7 %psum.30 = f32[4096]{0:T(1024)S(1)} all-reduce(f32[4096]{0:T(1024)S(1)} %maximum_multiply_fusion.2), channel_id=1, replica_groups=mesh['row'=16,'col'=16] {'col'}, use_global_device_ids=true, to_apply=%region_37.38 | all-reduce | flops 4096 | bytes 32768 | tf_op jit(solution)/shard_map/psum | solution.py:69
  (251 shorter events, 123.8 us)
Async XLA Ops:
  86.5 27.0 %copy-start = (bf16[2048,64]{0,1:T(8,128)(2,1)S(1)}, bf16[2048,64]{0,1:T(8,128)(2,1)}, u32[]{:S(2)}) copy-start(bf16[2048,64]{0,1:T(8,128)(2,1)} %param.17) | copy-start | bytes 786436
  86.6 27.1 %copy-start.1 = (bf16[2048]{0:T(1024)(128)(2,1)S(1)}, bf16[2048]{0:T(1024)(128)(2,1)}, u32[]{:S(2)}) copy-start(bf16[2048]{0:T(1024)(128)(2,1)} %param.19) | copy-start | bytes 12292
  220.2 180.3 %copy-start.2 = (bf16[2048]{0:T(1024)(128)(2,1)S(1)}, bf16[2048]{0:T(1024)(128)(2,1)}, u32[]{:S(2)}) copy-start(bf16[2048]{0:T(1024)(128)(2,1)} %param.18) | copy-start | bytes 12292
where the time goes:
time: 825 us; the launch traced here: 824 us
  blocking collectives  682 us (83%)
  other arithmetic  70.6 us (9%)
  matrix products  65.9 us (8%)
    pmax x2, blocking collectives, reduce_col(): merged_top = lax.pmax(maxima, 'col')  153 us
    psum x2, blocking collectives, reduce_col(): merged_total = lax.psum(totals * jnp.exp(maxima - merged_top), 'col')  153 us
    psum x2, blocking collectives, reduce_row(): merged_total = lax.psum(totals * jnp.exp(maxima - merged_top), 'row')  106 us
    pmax x2, blocking collectives, reduce_row(): merged_top = lax.pmax(maxima, 'row')  106 us
    dot_general x24, matrix products, advance(): lax.dot_general(piece_desc, right_desc, (((1,), (1,)), ((), ())), preferr...  65.9 us
    reduce_sum x20, other arithmetic, advance(): row_total = jnp.sum(jnp.exp(row_score - row_top[:, None]), axis=1)  56.8 us
    all_gather x1, blocking collectives, body(): source_rows = lax.all_gather(source_desc, 'col', axis=1, tiled=True)  47.2 us
    all_gather x1, blocking collectives, body(): lax.all_gather(target_mass_piece, 'col', axis=0, tiled=True)  39.8 us

commit v1 on v0

--- a/solution.py
+++ b/solution.py
@@ -97,7 +97,10 @@
     )
     target_rows, target_row_mass = (
         lax.all_gather(target_piece, "col", axis=0, tiled=True),
-        lax.all_gather(target_mass_piece, "col", axis=0, tiled=True),
+        jnp.concatenate(
+            lax.all_to_all(jnp.stack([target_mass_piece] * lax.axis_size("col")), "col", 0, 0),
+            axis=0,
+        ),
     )
     source_log = jnp.log(source_mass.astype(jnp.float32))
     source_col_log = jnp.log(source_col_mass.astype(jnp.float32))

time: 825 us -> 800 us (0.970)
  blocking collectives: 682 us -> 642 us
  starting transfers between devices: 0 us -> 10.1 us
    all_gather x1 -> x0, blocking collectives: 39.8 us -> none  [body(): lax.all_gather(target_mass_piece, 'col', axis=0, tiled=True)]
    all_to_all x0 -> x1, starting transfers between devices: none -> 10.1 us  [body(): lax.all_to_all(jnp.stack([target_mass_piece] * lax.axis_size('col')), 'co...]
  transfers between devices with their start and end apart: 0 -> 1, of which waited for: 0 -> 0; matrix products, arithmetic and copies ran while one was open for 0% -> 7% of each run, Pallas kernels for 0% -> 0%
where the time goes in v1:
time: 800 us; the launch traced here: 799 us
  blocking collectives  642 us (80%)
  other arithmetic  72.2 us (9%)
  matrix products  65.9 us (8%)
  starting transfers between devices  10.1 us (1%)
    pmax x2, blocking collectives, reduce_col(): merged_top = lax.pmax(maxima, 'col')  156 us
    psum x2, blocking collectives, reduce_col(): merged_total = lax.psum(totals * jnp.exp(maxima - merged_top), 'col')  153 us
    psum x2, blocking collectives, reduce_row(): merged_total = lax.psum(totals * jnp.exp(maxima - merged_top), 'row')  106 us
    pmax x2, blocking collectives, reduce_row(): merged_top = lax.pmax(maxima, 'row')  106 us
    dot_general x24, matrix products, advance(): lax.dot_general(piece_desc, right_desc, (((1,), (1,)), ((), ())), preferr...  65.9 us
    reduce_sum x20, other arithmetic, advance(): row_total = jnp.sum(jnp.exp(row_score - row_top[:, None]), axis=1)  56.7 us
    all_gather x1, blocking collectives, body(): source_rows = lax.all_gather(source_desc, 'col', axis=1, tiled=True)  46 us
    all_gather x1, blocking collectives, body(): lax.all_gather(target_piece, 'col', axis=0, tiled=True)  39.3 us
  transfers between devices with their start and end apart: 1, of which 0 were waited for; matrix products, arithmetic and copies ran while one was open for 7% of the time, Pallas kernels for 0%

profile of v1, /device:TPU:32, one launch (start us, length us, event | category | flops | bytes accessed | tf_op | source)
XLA Modules:
  0.0 798.9 jit_solution(2023481527729715888)
XLA Ops:
  2.0 10.1 %all-to-all-start = ((bf16[16,1,128]{2,1,0:T(2,128)(2,1)}), bf16[16,1,128]{2,1,0:T(2,128)(2,1)S(1)}, u32[]{:S(2)}, u32[]{:S(2)}) async-start(bf16[16,1,128]{2,1,0:T(2,128)(2,1)} %stack.2), calls=%async_computation | async-start | bytes 16384 | tf_op jit(solution)/shard_map/all_to_all | solution.py:101
  12.1 46.0 %all-gather = bf16[16,4,2048]{2,1,0:T(4,128)(2,1)S(1)} all-gather(bf16[1,4,2048]{2,1,0:T(4,128)(2,1)} %bitcast.204), channel_id=1, replica_groups=mesh['row'=16,'col'=16] {'col'}, dimensions={0}, use_global_device_ids=true | all-gather | bytes 278528 | tf_op jit(solution)/shard_map/all_gather | solution.py:88
  58.2 19.8 %all_gather.13 = bf16[2048,64]{0,1:T(8,128)(2,1)S(1)} all-gather(bf16[128,64]{0,1:T(8,128)(2,1)S(1)} %dynamic-slice_bitcast_fusion), channel_id=1, replica_groups=mesh['row'=16,'col'=16] {'row'}, dimensions={0}, use_global_device_ids=true | all-gather | bytes 278528 | tf_op jit(solution)/shard_map/all_gather | solution.py:91
  82.4 16.1 %all-gather.1 = bf16[16,1,128]{2,1,0:T(2,128)(2,1)S(1)} all-gather(bf16[1,1,128]{2,1,0:T(2,128)(2,1)S(1)} %dynamic-slice_bitcast_fusion.1), channel_id=1, replica_groups=mesh['row'=16,'col'=16] {'row'}, dimensions={0}, use_global_device_ids=true | all-gather | bytes 4352 | tf_op jit(solution)/shard_map/all_gather | solution.py:92
  98.9 26.9 %while.95 = (s32[]{:T(128)}, f32[2048]{0:T(1024)S(1)}, f32[2048]{0:T(1024)S(1)}, f32[4,512]{1,0:T(4,128)S(1)}, f32[4,512]{1,0:T(4,128)S(1)}, /*index=5*/f32[4,51...) while((s32[]{:T(128)}, f32[2048]{0:T(1024)S(1)}, ...), condition=%wide.region_14.15_spmd.clone, body=%wide.region_9.14_spmd.clone.sunk | while | flops 147858432 | bytes 9203864 | solution.py:61
  102.1 3.4 exponential_reduce_fusion.18
  108.8 3.4 exponential_reduce_fusion.18
  115.6 3.4 exponential_reduce_fusion.18
  122.3 3.4 exponential_reduce_fusion.18
  125.9 26.7 %while.94 = (s32[]{:T(128)}, f32[2048]{0:T(1024)S(1)}, f32[2048]{0:T(1024)S(1)}, f32[4,512]{1,0:T(4,128)S(1)}, f32[4,512]{1,0:T(4,128)S(1)}, /*index=5*/f32[4,51...) while((s32[]{:T(128)}, f32[2048]{0:T(1024)S(1)}, ...), condition=%wide.region_7.8_spmd.clone, body=%wide.region_2.7_spmd.clone.sunk | while | flops 147858432 | bytes 8941720 | solution.py:61
  129.1 3.4 exponential_reduce_fusion.17
  152.6 39.3 %all_gather.15 = bf16[2048,64]{0,1:T(8,128)(2,1)S(1)} all-gather(bf16[128,64]{0,1:T(8,128)(2,1)S(1)} %constant_dynamic-slice_fusion.11), channel_id=1, replica_groups=mesh['row'=16,'col'=16] {'col'}, dimensions={0}, use_global_device_ids=true | all-gather | bytes 278528 | tf_op jit(solution)/shard_map/all_gather | solution.py:99
  192.6 26.7 %while.96 = (s32[]{:T(128)}, f32[2048]{0:T(1024)S(1)}, f32[2048]{0:T(1024)S(1)}, f32[4,512]{1,0:T(4,128)S(1)}, f32[4,512]{1,0:T(4,128)S(1)}, /*index=5*/f32[4,51...) while((s32[]{:T(128)}, f32[2048]{0:T(1024)S(1)}, ...), condition=%wide.region_21.22_spmd.clone, body=%wide.region_16.21_spmd.clone.sunk | while | flops 147858432 | bytes 8941720 | solution.py:61
  219.3 78.8 %pmax.28 = f32[6144]{0:T(1024)S(1)} all-reduce(f32[6144]{0:T(1024)S(1)} %constant_dynamic-update-slice_fusion.8), channel_id=1, replica_groups=mesh['row'=16,'col'=16] {'col'}, use_global_device_ids=true, to_apply=%region_22.23 | all-reduce | flops 6144 | bytes 49152 | tf_op jit(solution)/shard_map/pmax | solution.py:68
  298.2 76.7 %psum.28 = f32[6144]{0:T(1024)S(1)} all-reduce(f32[6144]{0:T(1024)S(1)} %maximum_multiply_fusion), channel_id=1, replica_groups=mesh['row'=16,'col'=16] {'col'}, use_global_device_ids=true, to_apply=%region_23.24 | all-reduce | flops 6144 | bytes 49152 | tf_op jit(solution)/shard_map/psum | solution.py:69
  375.0 22.8 %while.98 = (s32[]{:T(128)}, f32[2048]{0:T(1024)S(1)}, f32[2048]{0:T(1024)S(1)}, f32[4,512]{1,0:T(4,128)S(1)}, f32[4,512]{1,0:T(4,128)S(1)}, /*index=5*/f32[2048...) while((s32[]{:T(128)}, f32[2048]{0:T(1024)S(1)}, ...), condition=%wide.region_41.42_spmd.clone, body=%wide.region_38.0_spmd.clone.sunk | while | flops 141568000 | bytes 8908920 | solution.py:61
  397.8 53.0 %pmax.29 = f32[6144]{0:T(1024)S(1)} all-reduce(f32[6144]{0:T(1024)S(1)} %constant_dynamic-update-slice_fusion.9), channel_id=1, replica_groups=mesh['row'=16,'col'=16] {'row'}, use_global_device_ids=true, to_apply=%region_24.25 | all-reduce | flops 6144 | bytes 49152 | tf_op jit(solution)/shard_map/pmax | solution.py:74
  450.8 53.1 %psum.29 = f32[6144]{0:T(1024)S(1)} all-reduce(f32[6144]{0:T(1024)S(1)} %maximum_multiply_fusion.1), channel_id=1, replica_groups=mesh['row'=16,'col'=16] {'row'}, use_global_device_ids=true, to_apply=%region_25.26 | all-reduce | flops 6144 | bytes 49152 | tf_op jit(solution)/shard_map/psum | solution.py:75
  504.0 26.7 %while.97 = (s32[]{:T(128)}, f32[2048]{0:T(1024)S(1)}, f32[2048]{0:T(1024)S(1)}, f32[4,512]{1,0:T(4,128)S(1)}, f32[4,512]{1,0:T(4,128)S(1)}, /*index=5*/f32[4,51...) while((s32[]{:T(128)}, f32[2048]{0:T(1024)S(1)}, ...), condition=%wide.region_31.32_spmd.clone, body=%wide.region_26.31_spmd.clone.sunk | while | flops 147858432 | bytes 8941720 | solution.py:61
  530.7 52.9 %pmax.31 = f32[4096]{0:T(1024)S(1)} all-reduce(f32[4096]{0:T(1024)S(1)} %constant_dynamic-update-slice_fusion.3), channel_id=1, replica_groups=mesh['row'=16,'col'=16] {'row'}, use_global_device_ids=true, to_apply=%region_42.43 | all-reduce | flops 4096 | bytes 32768 | tf_op jit(solution)/shard_map/pmax | solution.py:74
  583.7 52.9 %psum.31 = f32[4096]{0:T(1024)S(1)} all-reduce(f32[4096]{0:T(1024)S(1)} %maximum_multiply_fusion.3), channel_id=1, replica_groups=mesh['row'=16,'col'=16] {'row'}, use_global_device_ids=true, to_apply=%region_43.44 | all-reduce | flops 4096 | bytes 32768 | tf_op jit(solution)/shard_map/psum | solution.py:75
  637.2 7.4 while.93
  644.7 76.8 %pmax.30 = f32[4096]{0:T(1024)S(1)} all-reduce(f32[4096]{0:T(1024)S(1)} %constant_dynamic-update-slice_fusion.2), channel_id=1, replica_groups=mesh['row'=16,'col'=16] {'col'}, use_global_device_ids=true, to_apply=%region_36.37 | all-reduce | flops 4096 | bytes 32768 | tf_op jit(solution)/shard_map/pmax | solution.py:68
  721.5 76.7 %psum.30 = f32[4096]{0:T(1024)S(1)} all-reduce(f32[4096]{0:T(1024)S(1)} %maximum_multiply_fusion.2), channel_id=1, replica_groups=mesh['row'=16,'col'=16] {'col'}, use_global_device_ids=true, to_apply=%region_37.38 | all-reduce | flops 4096 | bytes 32768 | tf_op jit(solution)/shard_map/psum | solution.py:69
  (254 shorter events, 127.4 us)
Async XLA Ops:
  2.0 190.5 %all-to-all-start = ((bf16[16,1,128]{2,1,0:T(2,128)(2,1)}), bf16[16,1,128]{2,1,0:T(2,128)(2,1)S(1)}, u32[]{:S(2)}, u32[]{:S(2)}) async-start(bf16[16,1,128]{2,1,0:T(2,128)(2,1)} %stack.2), calls=%async_computation | async-start | bytes 16384 | tf_op jit(solution)/shard_map/all_to_all | solution.py:101
  98.9 27.0 %copy-start = (bf16[2048,64]{0,1:T(8,128)(2,1)S(1)}, bf16[2048,64]{0,1:T(8,128)(2,1)}, u32[]{:S(2)}) copy-start(bf16[2048,64]{0,1:T(8,128)(2,1)} %param.17) | copy-start | bytes 786436
  192.6 182.4 %copy-start.1 = (bf16[2048]{0:T(1024)(128)(2,1)S(1)}, bf16[2048]{0:T(1024)(128)(2,1)}, u32[]{:S(2)}) copy-start(bf16[2048]{0:T(1024)(128)(2,1)} %param.18) | copy-start | bytes 12292
  375.0 128.9 %copy-start.2 = (bf16[2048]{0:T(1024)(128)(2,1)S(1)}, bf16[2048]{0:T(1024)(128)(2,1)}, u32[]{:S(2)}) copy-start(bf16[2048]{0:T(1024)(128)(2,1)} %param.19) | copy-start | bytes 12292
